TPU v7x, 32 devices: a whole 2x2x4 slice. The times are simulated.
32 devices in a mesh: slab: 1, il: 32 (over z, y, x, core).
Axes of the slice: x: 2, y: 2, z: 4, core: 2. Of those that a mesh axis runs over, the one named last changes fastest.
Arguments:
- data: float32 [512, 128, 256], P(('slab', 'il')), may hold values from -100 to 100
- model: float32 [512, 128, 256], P(('slab', 'il')), may hold values from -6 to 6
- dip: int32 [512, 128, 256], P(('slab', 'il')), may hold values from 0 to 32
Outputs:
- new_model: float32 [512, 128, 256], P(('slab', 'il'))
- new_residual: float32 [512, 128, 256], P(('slab', 'il'))
All inputs are finite; a program needn't handle non-finite values.
Results may differ from a plain program's by a relative error of at most 0.000062.
Values sent between devices are 32-bit elements; how exact they have to be, the bound alone decides.
A program may use at most 128 MiB of HBM per device.

v0:
```python
import jax
import jax.numpy as jnp
from jax import lax
from jax.sharding import PartitionSpec as P

RAD = 64
NBINS = 33


def shifted(x, axis, by):
    devices = lax.axis_size(axis)
    pairs = [(i, i + by) for i in range(devices) if 0 <= i + by < devices]
    return lax.ppermute(x, axis, pairs)


def tent(offset):
    gap = jnp.abs(offset).astype(jnp.float32)
    return jnp.where(gap < RAD, (RAD - gap) / (RAD * RAD), 0.0)


def smooth_columns(volume):
    places = jnp.arange(volume.shape[1])
    weights = tent(places[:, None] - places[None, :])
    return jnp.einsum("xy,iyt->ixt", weights, volume, precision=lax.Precision.HIGHEST)


def coefficients(slopes):
    half = (NBINS - 1) / 2.0
    slope = (slopes.astype(jnp.float32) - half) / half
    return (slope * (slope - 1.0) / 2.0, 1.0 - slope * slope, slope * (slope + 1.0) / 2.0)


def destruct(volume, slopes):
    weight_early, weight_now, weight_late = coefficients(slopes)
    below = shifted(volume[-1:], "il", 1)
    previous = jnp.concatenate([below, volume[:-1]], 0)
    earlier = jnp.pad(previous, ((0, 0), (0, 0), (1, 0)))[:, :, :-1]
    later = jnp.pad(previous, ((0, 0), (0, 0), (0, 1)))[:, :, 1:]
    return volume - (weight_early * earlier + weight_now * previous + weight_late * later)


def transpose_destruct(residual, slopes):
    weight_early, weight_now, weight_late = coefficients(slopes)
    spread = weight_now * residual
    spread = spread + jnp.pad(weight_early * residual, ((0, 0), (0, 0), (0, 1)))[:, :, 1:]
    spread = spread + jnp.pad(weight_late * residual, ((0, 0), (0, 0), (1, 0)))[:, :, :-1]
    above = shifted(spread[:1], "il", -1)
    following = jnp.concatenate([spread[1:], above], 0)
    return residual - following


def smooth_inline_rim(gradient):
    count = gradient.shape[0]
    flat_shape = (count, -1)
    out_rows = jnp.arange(count)[:, None]
    in_rows = jnp.arange(count)[None, :]
    total = jnp.dot(
        tent(out_rows - in_rows), gradient.reshape(flat_shape), precision=lax.Precision.HIGHEST
    )
    reaches = (RAD - 1 + count - 1) // count
    for distance in range(1, reaches + 1):
        lower = shifted(gradient, "il", distance)
        upper = shifted(gradient, "il", -distance)
        total = total + jnp.dot(
            tent(out_rows - in_rows + distance * count),
            lower.reshape(flat_shape),
            precision=lax.Precision.HIGHEST,
        )
        total = total + jnp.dot(
            tent(out_rows - in_rows - distance * count),
            upper.reshape(flat_shape),
            precision=lax.Precision.HIGHEST,
        )
    return total.reshape(gradient.shape)


def local(data, model, dip):
    residual = data - destruct(model, dip)
    gradient = transpose_destruct(residual, dip)
    smoothed = smooth_inline_rim(gradient)
    shaped = smooth_columns(smoothed)
    image = destruct(shaped, dip)
    along, energy, length = lax.psum(
        (jnp.sum(gradient * shaped), jnp.sum(image * image), jnp.sum(shaped * shaped)), "il"
    )
    alpha = along / (energy + length)
    return (model + alpha * shaped, residual - alpha * image)


def solution(mesh):
    placed = (
        P(("slab", "il"), None, None),
        P(("slab", "il"), None, None),
        P(("slab", "il"), None, None),
    )
    return jax.shard_map(
        local,
        mesh=mesh,
        in_specs=placed,
        out_specs=(P(("slab", "il"), None, None), P(("slab", "il"), None, None)),
        check_vma=False,
    )
```

profile of v0, /device:TPU:0, one launch (start us, length us, event | category | flops | bytes accessed | tf_op | source)
XLA Modules:
  0.0 391.6 jit_solution(10598753732741858035)
XLA Ops:
  2.6 2.4 collective-permute-start
  5.0 2.9 copy.14
  7.8 3.0 copy.18
  13.1 3.2 fusion.15
  19.2 3.9 collective-permute-done.1
  24.7 6.8 %collective-permute-start.2 = (f32[16,128,256]{1,2,0:T(8,128)}, f32[16,128,256]{1,2,0:T(8,128)}, u32[]{:S(2)}, u32[]{:S(2)}) collective-permute-start(f32[16,128,256]{1,2,0:T(8,128)} %maximum_subtract_fusion), channel_id=1, source_target_pairs={{0,1},{1,2},{2,3},{3,4},{4,5},{5,6},{6,7},{7,8},{8,9},{9,10},{10,1... | collective-permute-start | bytes 6291464 | tf_op jit(solution)/shard_map/ppermute | solution.py:13
  32.8 5.0 %collective-permute-start.4 = (f32[16,128,256]{1,2,0:T(8,128)}, f32[16,128,256]{1,2,0:T(8,128)}, u32[]{:S(2)}, u32[]{:S(2)}) collective-permute-start(f32[16,128,256]{1,2,0:T(8,128)} %maximum_subtract_fusion), channel_id=1, source_target_pairs={{0,2},{1,3},{2,4},{3,5},{4,6},{5,7},{6,8},{7,9},{8,10},{9,11},{10,... | collective-permute-start | bytes 6291464 | tf_op jit(solution)/shard_map/ppermute | solution.py:13
  39.1 5.4 %collective-permute-start.6 = (f32[16,128,256]{1,2,0:T(8,128)}, f32[16,128,256]{1,2,0:T(8,128)}, u32[]{:S(2)}, u32[]{:S(2)}) collective-permute-start(f32[16,128,256]{1,2,0:T(8,128)} %maximum_subtract_fusion), channel_id=1, source_target_pairs={{0,3},{1,4},{2,5},{3,6},{4,7},{5,8},{6,9},{7,10},{8,11},{9,12},{10... | collective-permute-start | bytes 6291464 | tf_op jit(solution)/shard_map/ppermute | solution.py:13
  45.8 97.4 %collective-permute-start.8 = (f32[16,128,256]{1,2,0:T(8,128)}, f32[16,128,256]{1,2,0:T(8,128)}, u32[]{:S(2)}, u32[]{:S(2)}) collective-permute-start(f32[16,128,256]{1,2,0:T(8,128)} %maximum_subtract_fusion), channel_id=1, source_target_pairs={{0,4},{1,5},{2,6},{3,7},{4,8},{5,9},{6,10},{7,11},{8,12},{9,13},{1... | collective-permute-start | bytes 6291464 | tf_op jit(solution)/shard_map/ppermute | solution.py:13
  143.2 18.1 %collective-permute-done.4 = f32[16,128,256]{1,2,0:T(8,128)} collective-permute-done((f32[16,128,256]{1,2,0:T(8,128)}, f32[16,128,256]{1,2,0:T(8,128)}, u32[]{:S(2)}, u32[]{:S(2)}) %collective-permute-start.4) | collective-permute-done | bytes 2097184 | tf_op jit(solution)/shard_map/ppermute | solution.py:13
  162.6 3.1 copy.33
  165.7 4.8 %fusion.77 = f32[16,32768]{1,0:T(8,128)} fusion(f32[16,32768]{1,0:T(8,128)} %bitcast.54), kind=kOutput, calls=%fused_computation.113 | convolution fusion | flops 100665088 | bytes 4194304 | tf_op jit(solution)/shard_map/dot_general | solution.py:57
  170.5 3.0 copy.34
  173.5 3.0 copy.35
  176.6 3.1 copy.36
  179.6 4.9 %collective-permute-done.5 = f32[16,128,256]{1,2,0:T(8,128)} collective-permute-done((f32[16,128,256]{1,2,0:T(8,128)}, f32[16,128,256]{1,2,0:T(8,128)}, u32[]{:S(2)}, u32[]{:S(2)}) %collective-permute-start.5) | collective-permute-done | bytes 2097184 | tf_op jit(solution)/shard_map/ppermute | solution.py:13
  184.5 3.1 copy.37
  187.6 23.0 %collective-permute-done.6 = f32[16,128,256]{1,2,0:T(8,128)} collective-permute-done((f32[16,128,256]{1,2,0:T(8,128)}, f32[16,128,256]{1,2,0:T(8,128)}, u32[]{:S(2)}, u32[]{:S(2)}) %collective-permute-start.6) | collective-permute-done | bytes 2097184 | tf_op jit(solution)/shard_map/ppermute | solution.py:13
  210.7 3.1 copy.38
  213.7 10.4 %collective-permute-done.7 = f32[16,128,256]{1,2,0:T(8,128)} collective-permute-done((f32[16,128,256]{1,2,0:T(8,128)}, f32[16,128,256]{1,2,0:T(8,128)}, u32[]{:S(2)}, u32[]{:S(2)}) %collective-permute-start.7) | collective-permute-done | bytes 2097184 | tf_op jit(solution)/shard_map/ppermute | solution.py:13
  224.1 3.0 copy.39
  227.2 31.7 %collective-permute-done.8 = f32[16,128,256]{1,2,0:T(8,128)} collective-permute-done((f32[16,128,256]{1,2,0:T(8,128)}, f32[16,128,256]{1,2,0:T(8,128)}, u32[]{:S(2)}, u32[]{:S(2)}) %collective-permute-start.8) | collective-permute-done | bytes 2097184 | tf_op jit(solution)/shard_map/ppermute | solution.py:13
  258.9 3.1 copy.40
  262.0 3.1 copy.41
  265.0 4.3 %convolution_add_fusion.7 = f32[16,32768]{1,0:T(8,128)S(1)} fusion(f32[16,32768]{1,0:T(8,128)} %fusion.77, f32[16,32768]{1,0:T(8,128)} %bitcast.45), kind=kOutput, calls=%fused_computation.7 | convolution fusion | flops 101189632 | bytes 6291456 | tf_op jit(solution)/shard_map/dot_general | solution.py:64
  279.2 2.2 convolution_add_fusion.1
  283.9 3.5 convolution_bitcast_fusion
  287.5 5.4 %collective-permute-start.10 = (f32[1,128,256]{1,2,0:T(8,128)S(1)}, f32[1,128,256]{1,2,0:T(8,128)S(1)}, u32[]{:S(2)}, u32[]{:S(2)}) collective-permute-start(f32[1,128,256]{1,2,0:T(8,128)S(1)} %slice.52), channel_id=1, source_target_pairs={{0,1},{1,2},{2,3},{3,4},{4,5},{5,6},{6,7},{7,8},{8,9},{9,10},{10,1... | collective-permute-start | bytes 393224 | tf_op jit(solution)/shard_map/ppermute | solution.py:13
  294.6 4.8 %multiply_reduce_fusion.1 = (f32[]{:T(128)}, f32[16,128,256]{1,2,0:T(8,128)}, f32[]{:T(128)}, f32[]{:T(128)}) fusion(f32[16,128,256]{1,2,0:T(8,128)S(1)} %convolution_bitcast_fusion, f32[16,128,256]{1,2,0:T(8,128)S(1)} %pad_maximum_fusion.1, s32[16,128,256]{1,2,0:T(8,128)S(1)} %copy-done.1, f32[16,128,256]{1,2,0:T(8,128)} %maximum_subtract_fusion), kind=kLoop, calls=%fused_computation.37 | loop fusion | flops 12058621 | bytes 10485772 | tf_op jit(solution)/shard_map/reduce_sum | solution.py:84
  300.6 79.1 %all-reduce.6 = (f32[]{:T(128)}, f32[]{:T(128)}) all-reduce(f32[]{:T(128)} %get-tuple-element.14, f32[]{:T(128)S(6)} %add.108), channel_id=1, replica_groups=mesh['slab'=1,'il'=32] {'il'}, use_global_device_ids=true, to_apply=%region_1.2 | all-reduce | flops 2 | bytes 16 | tf_op jit(solution)/shard_map/psum | solution.py:83
  381.0 5.7 %multiply_subtract_fusion = (f32[16,128,256]{1,2,0:T(8,128)}, f32[16,128,256]{1,2,0:T(8,128)}) fusion(f32[16,128,256]{1,2,0:T(8,128)S(1)} %get-tuple-element.13, f32[16,128,256]{1,2,0:T(8,128)} %get-tuple-element.11, f32[]{:T(128)S(6)} %div.65, f32[16,128,256]{1,2,0:T(8,128)} %copy-done.2, f32[16,128,256]{1,2,0:T(8,128)} %copy-done.4), kind=kLoop, calls=%fused_computation.34 | loop fusion | flops 2097152 | bytes 12582916 | tf_op jit(solution)/shard_map/sub | solution.py:87
  386.8 3.0 copy.30
  (57 shorter events, 29.6 us)
Async XLA Ops:
  2.5 2.4 copy-start.2
  2.6 8.3 %collective-permute-start = (f32[1,128,256]{1,2,0:T(8,128)S(1)}, f32[1,128,256]{1,2,0:T(8,128)S(1)}, u32[]{:S(2)}, u32[]{:S(2)}) collective-permute-start(f32[1,128,256]{1,2,0:T(8,128)S(1)} %slice.48), channel_id=1, source_target_pairs={{0,1},{1,2},{2,3},{3,4},{4,5},{5,6},{6,7},{7,8},{8,9},{9,10},{10,1... | collective-permute-start | bytes 393224 | tf_op jit(solution)/shard_map/ppermute | solution.py:13
  7.8 3.0 slice-start
  10.9 1.6 copy-start
  10.9 2.2 copy-start.3
  17.8 5.3 %collective-permute-start.1 = (f32[1,128,256]{1,2,0:T(8,128)S(1)}, f32[1,128,256]{1,2,0:T(8,128)S(1)}, u32[]{:S(2)}, u32[]{:S(2)}) collective-permute-start(f32[1,128,256]{1,2,0:T(8,128)S(1)} %slice.51), channel_id=1, source_target_pairs={{1,0},{2,1},{3,2},{4,3},{5,4},{6,5},{7,6},{8,7},{9,8},{10,9},{11,1... | collective-permute-start | bytes 393224 | tf_op jit(solution)/shard_map/ppermute | solution.py:13
  24.7 19.7 %collective-permute-start.2 = (f32[16,128,256]{1,2,0:T(8,128)}, f32[16,128,256]{1,2,0:T(8,128)}, u32[]{:S(2)}, u32[]{:S(2)}) collective-permute-start(f32[16,128,256]{1,2,0:T(8,128)} %maximum_subtract_fusion), channel_id=1, source_target_pairs={{0,1},{1,2},{2,3},{3,4},{4,5},{5,6},{6,7},{7,8},{8,9},{9,10},{10,1... | collective-permute-start | bytes 6291464 | tf_op jit(solution)/shard_map/ppermute | solution.py:13
  31.5 14.2 %collective-permute-start.3 = (f32[16,128,256]{1,2,0:T(8,128)}, f32[16,128,256]{1,2,0:T(8,128)}, u32[]{:S(2)}, u32[]{:S(2)}) collective-permute-start(f32[16,128,256]{1,2,0:T(8,128)} %maximum_subtract_fusion), channel_id=1, source_target_pairs={{1,0},{2,1},{3,2},{4,3},{5,4},{6,5},{7,6},{8,7},{9,8},{10,9},{11,1... | collective-permute-start | bytes 6291464 | tf_op jit(solution)/shard_map/ppermute | solution.py:13
  32.8 128.5 %collective-permute-start.4 = (f32[16,128,256]{1,2,0:T(8,128)}, f32[16,128,256]{1,2,0:T(8,128)}, u32[]{:S(2)}, u32[]{:S(2)}) collective-permute-start(f32[16,128,256]{1,2,0:T(8,128)} %maximum_subtract_fusion), channel_id=1, source_target_pairs={{0,2},{1,3},{2,4},{3,5},{4,6},{5,7},{6,8},{7,9},{8,10},{9,11},{10,... | collective-permute-start | bytes 6291464 | tf_op jit(solution)/shard_map/ppermute | solution.py:13
  37.8 146.8 %collective-permute-start.5 = (f32[16,128,256]{1,2,0:T(8,128)}, f32[16,128,256]{1,2,0:T(8,128)}, u32[]{:S(2)}, u32[]{:S(2)}) collective-permute-start(f32[16,128,256]{1,2,0:T(8,128)} %maximum_subtract_fusion), channel_id=1, source_target_pairs={{2,0},{3,1},{4,2},{5,3},{6,4},{7,5},{8,6},{9,7},{10,8},{11,9},{12,... | collective-permute-start | bytes 6291464 | tf_op jit(solution)/shard_map/ppermute | solution.py:13
  39.1 171.6 %collective-permute-start.6 = (f32[16,128,256]{1,2,0:T(8,128)}, f32[16,128,256]{1,2,0:T(8,128)}, u32[]{:S(2)}, u32[]{:S(2)}) collective-permute-start(f32[16,128,256]{1,2,0:T(8,128)} %maximum_subtract_fusion), channel_id=1, source_target_pairs={{0,3},{1,4},{2,5},{3,6},{4,7},{5,8},{6,9},{7,10},{8,11},{9,12},{10... | collective-permute-start | bytes 6291464 | tf_op jit(solution)/shard_map/ppermute | solution.py:13
  44.5 179.7 %collective-permute-start.7 = (f32[16,128,256]{1,2,0:T(8,128)}, f32[16,128,256]{1,2,0:T(8,128)}, u32[]{:S(2)}, u32[]{:S(2)}) collective-permute-start(f32[16,128,256]{1,2,0:T(8,128)} %maximum_subtract_fusion), channel_id=1, source_target_pairs={{3,0},{4,1},{5,2},{6,3},{7,4},{8,5},{9,6},{10,7},{11,8},{12,9},{13... | collective-permute-start | bytes 6291464 | tf_op jit(solution)/shard_map/ppermute | solution.py:13
  45.8 213.1 %collective-permute-start.8 = (f32[16,128,256]{1,2,0:T(8,128)}, f32[16,128,256]{1,2,0:T(8,128)}, u32[]{:S(2)}, u32[]{:S(2)}) collective-permute-start(f32[16,128,256]{1,2,0:T(8,128)} %maximum_subtract_fusion), channel_id=1, source_target_pairs={{0,4},{1,5},{2,6},{3,7},{4,8},{5,9},{6,10},{7,11},{8,12},{9,13},{1... | collective-permute-start | bytes 6291464 | tf_op jit(solution)/shard_map/ppermute | solution.py:13
  161.3 100.6 %collective-permute-start.9 = (f32[16,128,256]{1,2,0:T(8,128)}, f32[16,128,256]{1,2,0:T(8,128)}, u32[]{:S(2)}, u32[]{:S(2)}) collective-permute-start(f32[16,128,256]{1,2,0:T(8,128)} %maximum_subtract_fusion), channel_id=1, source_target_pairs={{4,0},{5,1},{6,2},{7,3},{8,4},{9,5},{10,6},{11,7},{12,8},{13,9},{1... | collective-permute-start | bytes 6291464 | tf_op jit(solution)/shard_map/ppermute | solution.py:13
  265.0 4.3 %copy-start.6 = (f32[2,8,128,256]{3,1,2,0:T(8,128)S(1)}, f32[2,8,128,256]{3,1,2,0:T(8,128)}, u32[]{:S(2)}) copy-start(f32[2,8,128,256]{3,1,2,0:T(8,128)} %copy.35) | copy-start | bytes 6291460
  269.4 2.0 copy-start.5
  271.3 2.0 copy-start.7
  273.3 2.0 copy-start.8
  275.3 2.0 copy-start.9
  277.2 2.0 copy-start.10
  279.2 2.2 copy-start.11
  287.4 6.5 %copy-start.4 = (f32[16,128,256]{1,2,0:T(8,128)}, f32[16,128,256]{1,2,0:T(8,128)S(1)}, u32[]{:S(2)}) copy-start(f32[16,128,256]{1,2,0:T(8,128)S(1)} %convolution_bitcast_fusion) | copy-start | bytes 6291460
  287.5 6.4 %collective-permute-start.10 = (f32[1,128,256]{1,2,0:T(8,128)S(1)}, f32[1,128,256]{1,2,0:T(8,128)S(1)}, u32[]{:S(2)}, u32[]{:S(2)}) collective-permute-start(f32[1,128,256]{1,2,0:T(8,128)S(1)} %slice.52), channel_id=1, source_target_pairs={{0,1},{1,2},{2,3},{3,4},{4,5},{5,6},{6,7},{7,8},{8,9},{9,10},{10,1... | collective-permute-start | bytes 393224 | tf_op jit(solution)/shard_map/ppermute | solution.py:13
  293.0 1.6 copy-start.1
  386.8 3.0 copy-start.12
where the time goes:
time: 392 us
  starting transfers between devices  129 us (33%)
  waiting for transfers between devices  92.9 us (24%)
  blocking collectives  79.1 us (20%)
  local copies, waits for them, and re-layouts  43.8 us (11%)
  matrix products  26.4 us (7%)
  other arithmetic  17 us (4%)
    ppermute x11, starting transfers between devices, shifted(): return lax.ppermute(x, axis, pairs)  129 us
    ppermute x11, waiting for transfers between devices, shifted(): return lax.ppermute(x, axis, pairs)  92.9 us
    psum x1, blocking collectives, local(): lax.psum((jnp.sum(gradient * shaped), jnp.sum(image * image), jnp.sum(sha...  79.1 us
    unnamed x41, local copies, waits for them, and re-layouts  43.5 us
    dot_general x4, matrix products, smooth_inline_rim(): jnp.dot(tent(out_rows - in_rows + distance * count), lower.reshape(flat_s...  10.3 us
  transfers between devices with their start and end apart: 11, of which 7 were waited for; matrix products, arithmetic and copies ran while one was open for 9% of the time, Pallas kernels for 0%

commit v1 on v0

v1 whole, which is shorter than its diff:
```python
import functools

import jax
import jax.numpy as jnp
import numpy as np
from jax import lax
from jax.experimental import pallas as pl
from jax.experimental.pallas import tpu as pltpu
from jax.sharding import PartitionSpec as P

RAD = 64
NBINS = 33
PARTS = 8


def at_lane(x, lane):
    return lax.broadcasted_iota(jnp.int32, x.shape, x.ndim - 1) == lane


def before(x):
    return jnp.where(at_lane(x, 0), 0.0, pltpu.roll(x, 1, x.ndim - 1))


def after(x):
    last = x.shape[-1] - 1
    return jnp.where(at_lane(x, last), 0.0, pltpu.roll(x, last, x.ndim - 1))


def coefficients(bins):
    half = (NBINS - 1) // 2
    slope = (bins - half).astype(jnp.float32) * (1.0 / half)
    square = slope * slope
    return 0.5 * (square - slope), 1.0 - square, 0.5 * (square + slope)


def predict(u, weights):
    early, now, late = weights
    return early * before(u) + now * u + late * after(u)


def spread(r, weights):
    early, now, late = weights
    return now * r + after(early * r) + before(late * r)


def kernel(n, data_hbm, model_hbm, dip_hbm, tents_ref, new_model, new_res,
           data, model, dip, res, grad, halo, sums_out, sums_in, split, shaped, image,
           below, above, above_dip, part, table, part_two, table_two,
           load_sem, edge_send, edge_recv, near_send, near_recv, far_send, far_recv,
           sum_send, sum_recv, one_send, one_recv, two_send, two_recv):
    count, columns, _ = data.shape
    width = columns // PARTS
    groups = n // 8
    me = lax.axis_index("il")
    pos = lax.rem(me, 8)
    group = lax.div(me, 8)
    side = lax.div(pos, 4)
    place = lax.rem(pos, 4)
    base8 = me - pos
    base4 = me - place
    toward = 1 - 2 * side
    partner = me + 4 * toward
    onward = me + 8 * toward
    origin = me - 8 * toward
    has_onward = jnp.logical_and(onward >= 0, onward < n)
    has_origin = jnp.logical_and(origin >= 0, origin < n)
    has_below = me > 0
    has_above = me < n - 1

    def remote(src, dst, send, recv, to):
        return pltpu.make_async_remote_copy(
            src_ref=src, dst_ref=dst, send_sem=send, recv_sem=recv,
            device_id={"il": to}, device_id_type=pl.DeviceIdType.MESH)

    loads = [pltpu.make_async_copy(src, dst, load_sem.at[i]) for i, (src, dst) in enumerate(
        ((data_hbm, data), (model_hbm, model), (dip_hbm, dip)))]
    for load in loads:
        load.start()

    barrier = pltpu.get_barrier_semaphore()

    def greet(other):
        pl.semaphore_signal(barrier, inc=1, device_id={"il": other},
                            device_id_type=pl.DeviceIdType.MESH)

    for o in range(1, 8):
        greet(base8 + lax.rem(pos + o, 8))
    for o in range(1, groups):
        greet(lax.rem(me + 8 * o, n))
    cross_below = jnp.logical_and(pos == 0, has_below)
    cross_above = jnp.logical_and(pos == 7, has_above)

    @pl.when(cross_below)
    def _():
        greet(me - 1)

    @pl.when(cross_above)
    def _():
        greet(me + 1)

    crossings = cross_below.astype(jnp.int32) + cross_above.astype(jnp.int32)
    pl.semaphore_wait(barrier, 7 + groups - 1 + crossings)

    def up():
        return [remote(model_hbm.at[count - 1], below, edge_send.at[0], edge_recv.at[0], me + 1)]

    def down():
        return [remote(src.at[0], dst, edge_send.at[i], edge_recv.at[i], me - 1)
                for i, src, dst in ((1, data_hbm, above.at[0]), (2, model_hbm, above.at[1]),
                                    (3, dip_hbm, above_dip))]

    @pl.when(has_above)
    def _():
        for copy in up():
            copy.start()

    @pl.when(has_below)
    def _():
        for copy in down():
            copy.start()

    for load in loads:
        load.wait()

    def strip(k):
        return pl.ds(pl.multiple_of(k * width, width), width)

    def own(k, carry):
        xs = strip(k)
        last = None
        for i in range(1, count):
            weights = coefficients(dip[i, xs])
            r = data[i, xs] - model[i, xs] + predict(model[i - 1, xs], weights)
            res[i, xs] = r
            s = spread(r, weights)
            grad[i - 1, xs] = -s if last is None else last - s
            last = r
        grad[count - 1, xs] = last
        return carry

    lax.fori_loop(0, PARTS, own, 0)

    @pl.when(has_below)
    def _():
        for copy in up():
            copy.wait_recv()

    @pl.when(jnp.logical_not(has_below))
    def _():
        below[...] = jnp.zeros_like(below)

    @pl.when(has_above)
    def _():
        for copy in down():
            copy.wait_recv()

    def edges(k, carry):
        xs = strip(k)
        r = data[0, xs] - model[0, xs] + predict(below[xs], coefficients(dip[0, xs]))
        res[0, xs] = r
        grad[0, xs] = grad[0, xs] + r

        @pl.when(has_above)
        def _():
            weights = coefficients(above_dip[xs])
            r = above[0, xs] - above[1, xs] + predict(model[count - 1, xs], weights)
            grad[count - 1, xs] = grad[count - 1, xs] - spread(r, weights)

        near(k).start()
        return carry

    def near(k):
        return remote(grad.at[:, strip(k)], halo.at[side, :, strip(k)],
                      near_send.at[k], near_recv.at[k], partner)

    def near_arrival(k):
        return remote(grad.at[:, strip(k)], halo.at[1 - side, :, strip(k)],
                      near_send.at[k], near_recv.at[k], partner)

    def far(k):
        return remote(halo.at[1 - side, :, strip(k)], halo.at[side, :, strip(k)],
                      far_send.at[k], far_recv.at[k], onward)

    def moments(o, k):
        return remote(sums_out.at[o - 1, :, strip(k)], sums_in.at[o - 1, :, strip(k)],
                      sum_send.at[o - 1, k], sum_recv.at[o - 1, k],
                      base4 + lax.rem(place + o, 4))

    lax.fori_loop(0, PARTS, edges, 0)

    @pl.when(jnp.logical_not(has_origin))
    def _():
        def clear(i, carry):
            halo[side, i] = jnp.zeros(halo.shape[2:], halo.dtype)
            return carry
        lax.fori_loop(0, count, clear, 0)

    def totals(rows):
        zero = rows[0]
        first = rows[1]
        for row in rows[2:]:
            first = first + row
        one = rows[1]
        for j in range(2, count):
            one = one + j * rows[j]
        return zero + first, one

    def send_moments(k):
        xs = strip(k)
        left0, left1 = totals([halo[0, j, xs] for j in range(count)])
        own0, own1 = totals([grad[j, xs] for j in range(count)])
        right0, right1 = totals([halo[1, j, xs] for j in range(count)])
        for o in range(1, 4):
            wrap = place + o >= 4
            a0 = jnp.where(wrap, left0, own0)
            a1 = jnp.where(wrap, left1, own1)
            b0 = jnp.where(wrap, own0, right0)
            b1 = jnp.where(wrap, own1, right1)
            sums_out[o - 1, 0, xs] = (RAD - count * o) * a0 + a1 + (count * o) * b0 - b1
            sums_out[o - 1, 1, xs] = b0 - a0
            moments(o, k).start()
        sums_out[3, 0, xs] = RAD * own0 - own1 + left1
        sums_out[3, 1, xs] = own0 - left0

    def smooth(k):
        xs = strip(k)
        for o in range(1, 4):
            moments(o, k).wait_recv()
        value = sums_out[3, 0, xs]
        step = sums_out[3, 1, xs]
        for o in range(3):
            value = value + sums_in[o, 0, xs]
            step = step + sums_in[o, 1, xs]
        low = pl.ds(pl.multiple_of(columns + k * width, width), width)

        def put(i, v):
            high = v.astype(jnp.bfloat16)
            split[i, xs] = high
            split[i, low] = (v - high.astype(jnp.float32)).astype(jnp.bfloat16)

        put(0, value - step)
        for i in range(count):
            put(i + 1, value)
            if i < count - 1:
                step = step + ((halo[0, i, xs] + halo[1, i, xs]) - 2.0 * grad[i, xs])
                value = value + step

    def stage(k, carry):
        @pl.when(k < PARTS)
        def _():
            near_arrival(k).wait_recv()

            @pl.when(has_onward)
            def _():
                far(k).start()

        @pl.when(jnp.logical_and(k >= 1, k <= PARTS))
        def _():
            @pl.when(has_origin)
            def _():
                far(k - 1).wait_recv()
            send_moments(k - 1)

        @pl.when(k >= 2)
        def _():
            smooth(k - 2)
        return carry

    lax.fori_loop(0, PARTS + 2, stage, 0)

    def across(i, carry):
        out = jnp.dot(tents_ref[...], split[i], preferred_element_type=jnp.float32)
        shaped[i] = jnp.where(jnp.logical_or(i > 0, has_below), out, 0.0)
        return carry

    lax.fori_loop(0, count + 1, across, 0)

    def fold(x):
        return jnp.sum(x.reshape(x.shape[0] // 8, 8, x.shape[1]), 0)

    def images(k, carry):
        xs = strip(k)
        along, energy, length = carry
        last = shaped[0, xs]
        for i in range(count):
            now = shaped[i + 1, xs]
            im = now - predict(last, coefficients(dip[i, xs]))
            image[i, xs] = im
            along = along + fold(grad[i, xs] * now)
            energy = energy + fold(im * im)
            length = length + fold(now * now)
            last = now
        return along, energy, length

    none = jnp.zeros((8, data.shape[2]), jnp.float32)
    sums = lax.fori_loop(0, PARTS, images, (none, none, none))
    row = lax.broadcasted_iota(jnp.int32, (8, 128), 0)
    tile = jnp.zeros((8, 128), jnp.float32)
    for q, total in enumerate(sums):
        flat = jnp.sum(total, 0, keepdims=True)
        flat = sum(flat[:, c:c + 128] for c in range(0, flat.shape[1], 128))
        tile = jnp.where(row == q, flat, tile)
    part[...] = tile
    table[pos] = tile

    def one(o):
        return remote(part, table.at[pos], one_send.at[o - 1], one_recv.at[o - 1],
                      base8 + lax.rem(pos + o, 8))

    def one_arrival(o):
        return remote(part, table.at[lax.rem(pos + 8 - o, 8)], one_send.at[o - 1],
                      one_recv.at[o - 1], base8 + lax.rem(pos + o, 8))

    def two(o):
        return remote(part_two, table_two.at[group], two_send.at[o - 1], two_recv.at[o - 1],
                      lax.rem(me + 8 * o, n))

    def two_arrival(o):
        return remote(part_two, table_two.at[lax.rem(group + groups - o, groups)],
                      two_send.at[o - 1], two_recv.at[o - 1], lax.rem(me + 8 * o, n))

    for o in range(1, 8):
        one(o).start()
    for o in range(1, 8):
        one_arrival(o).wait_recv()
    tile = table[0]
    for o in range(1, 8):
        tile = tile + table[o]
    part_two[...] = tile
    table_two[group] = tile
    for o in range(1, groups):
        two(o).start()
    for o in range(1, groups):
        two_arrival(o).wait_recv()
    tile = table_two[0]
    for o in range(1, groups):
        tile = tile + table_two[o]
    along, energy, length = (jnp.sum(tile[q:q + 1], 1, keepdims=True) for q in range(3))
    alpha = along / (energy + length)

    def update(i, carry):
        new_model[i] = model[i] + alpha * shaped[i + 1]
        new_res[i] = res[i] - alpha * image[i]
        return carry

    lax.fori_loop(0, count, update, 0)

    @pl.when(has_above)
    def _():
        for copy in up():
            copy.wait_send()

    @pl.when(has_below)
    def _():
        for copy in down():
            copy.wait_send()

    def finish(k, carry):
        near(k).wait_send()

        @pl.when(has_onward)
        def _():
            far(k).wait_send()
        for o in range(1, 4):
            moments(o, k).wait_send()
        return carry

    lax.fori_loop(0, PARTS, finish, 0)
    for o in range(1, 8):
        one(o).wait_send()
    for o in range(1, groups):
        two(o).wait_send()


def local(n, data, model, dip):
    count, columns, times = data.shape
    assert count * 4 == RAD and n % 8 == 0
    groups = n // 8
    gap = np.abs(np.arange(columns)[:, None] - np.arange(columns)[None, :])
    tent = np.maximum(RAD - gap, 0) / float(RAD) ** 4
    tents = jnp.asarray(np.concatenate([tent, tent], 1), jnp.bfloat16)
    block = (count, columns, times)
    f32 = jnp.float32
    dma = pltpu.SemaphoreType.DMA
    return pl.pallas_call(
        functools.partial(kernel, n),
        out_shape=[jax.ShapeDtypeStruct(block, f32)] * 2,
        in_specs=[pl.BlockSpec(memory_space=pl.ANY)] * 3
        + [pl.BlockSpec(memory_space=pltpu.VMEM)],
        out_specs=[pl.BlockSpec(memory_space=pltpu.VMEM)] * 2,
        scratch_shapes=[
            pltpu.VMEM(block, f32),
            pltpu.VMEM(block, f32),
            pltpu.VMEM(block, jnp.int32),
            pltpu.VMEM(block, f32),
            pltpu.VMEM(block, f32),
            pltpu.VMEM((2,) + block, f32),
            pltpu.VMEM((4, 2, columns, times), f32),
            pltpu.VMEM((3, 2, columns, times), f32),
            pltpu.VMEM((count + 1, 2 * columns, times), jnp.bfloat16),
            pltpu.VMEM((count + 1, columns, times), f32),
            pltpu.VMEM(block, f32),
            pltpu.VMEM((columns, times), f32),
            pltpu.VMEM((2, columns, times), f32),
            pltpu.VMEM((columns, times), jnp.int32),
            pltpu.VMEM((8, 128), f32),
            pltpu.VMEM((8, 8, 128), f32),
            pltpu.VMEM((8, 128), f32),
            pltpu.VMEM((groups, 8, 128), f32),
            dma((3,)),
            dma((4,)), dma((4,)),
            dma((PARTS,)), dma((PARTS,)),
            dma((PARTS,)), dma((PARTS,)),
            dma((3, PARTS)), dma((3, PARTS)),
            dma((7,)), dma((7,)),
            dma((max(groups - 1, 1),)), dma((max(groups - 1, 1),)),
        ],
        compiler_params=pltpu.CompilerParams(
            collective_id=0, has_side_effects=True, vmem_limit_bytes=48 * 2**20),
    )(data, model, dip, tents)


def solution(mesh):
    placed = P(("slab", "il"), None, None)
    return jax.shard_map(
        functools.partial(local, mesh.shape["il"]),
        mesh=mesh,
        in_specs=(placed, placed, placed),
        out_specs=(placed, placed),
        check_vma=False,
    )
```

time: 392 us -> 88.2 us (0.23)
  starting transfers between devices: 129 us -> 0 us
  waiting for transfers between devices: 92.9 us -> 0 us
  Pallas kernels: 0 us -> 83.9 us
  blocking collectives: 79.1 us -> 0 us
  local copies, waits for them, and re-layouts: 43.8 us -> 3.48 us
  matrix products: 26.4 us -> 0 us
  other arithmetic: 17 us -> 0 us
    ppermute x11 -> x0, starting transfers between devices: 129 us -> none  [shifted(): return lax.ppermute(x, axis, pairs)]
    ppermute x11 -> x0, waiting for transfers between devices: 92.9 us -> none  [shifted(): return lax.ppermute(x, axis, pairs)]
    pallas_call x0 -> x1, Pallas kernels: none -> 83.9 us  [local(): pl.pallas_call(functools.partial(kernel, n), out_shape=[jax.ShapeDtypeStr...]
    psum x1 -> x0, blocking collectives: 79.1 us -> none  [local(): lax.psum((jnp.sum(gradient * shaped), jnp.sum(image * image), jnp.sum(sha...]
    unnamed x41 -> x4, local copies, waits for them, and re-layouts: 43.5 us -> 3.48 us
    dot_general x10 -> x0, matrix products: 26.4 us -> none  [the longest x4 10.3 us: smooth_inline_rim(): jnp.dot(tent(out_rows - in_rows + distance * count), lower.reshape(flat_s...]
    sub x2 -> x0, other arithmetic: 7.32 us -> none  [the longest x1 5.73 us: local(): return (model + alpha * shaped, residual - alpha * image)]
    reduce_sum x1 -> x0, other arithmetic: 4.76 us -> none  [local(): jnp.sum(image * image)]
  transfers between devices with their start and end apart: 11 -> 0, of which waited for: 7 -> 0; matrix products, arithmetic and copies ran while one was open for 9% -> 0% of each run, Pallas kernels for 0% -> 0%
where the time goes in v1:
time: 88.2 us; the launch traced here: 88 us
  Pallas kernels  83.9 us (95%)
  local copies, waits for them, and re-layouts  3.48 us (4%)
    pallas_call x1, Pallas kernels, local(): pl.pallas_call(functools.partial(kernel, n), out_shape=[jax.ShapeDtypeStr...  83.9 us
    unnamed x4, local copies, waits for them, and re-layouts  3.48 us

profile of v1, /device:TPU:0, one launch (start us, length us, event | category | flops | bytes accessed | tf_op | source)
XLA Modules:
  0.0 88.0 jit_solution(212074634162390844)
XLA Ops:
  0.6 0.0 copy-start
  0.6 0.8 copy-done
  1.5 83.9 %shard_map.59 = (f32[16,128,256]{2,1,0:T(8,128)S(1)}, f32[16,128,256]{2,1,0:T(8,128)S(1)}) custom-call(f32[16,128,256]{2,1,0:T(8,128)} %data_hbm.1, f32[16,128,256]{2,1,0:T(8,128)} %model_hbm.1, s32[16,128,256]{2,1,0:T(8,128)} %dip_hbm.1, bf16[128,256]{1,0:T(8,128)(2,1)S(1)} %copy-done), custom_call_target="tpu_custom_call" | custom-call | tf_op jit(solution)/shard_map/pallas_call | solution.py:385
  85.4 1.3 %copy.8 = f32[16,128,256]{2,1,0:T(8,128)} copy(f32[16,128,256]{2,1,0:T(8,128)S(1)} %get-tuple-element.4) | data formatting | bytes 4194304
  86.7 1.3 %copy.9 = f32[16,128,256]{2,1,0:T(8,128)} copy(f32[16,128,256]{2,1,0:T(8,128)S(1)} %get-tuple-element.5) | data formatting | bytes 4194304
Async XLA Ops:
  0.6 0.8 copy-start

commit v2 on v1

--- a/solution.py
+++ b/solution.py
@@ -2,7 +2,6 @@
 
 import jax
 import jax.numpy as jnp
-import numpy as np
 from jax import lax
 from jax.experimental import pallas as pl
 from jax.experimental.pallas import tpu as pltpu
@@ -11,6 +10,14 @@
 RAD = 64
 NBINS = 33
 PARTS = 8
+GROUP = 8
+EARLY = 1
+PIECES = 4
+
+
+def pieces(count):
+    third = (count - 2 + 2) // 3
+    return ((2, third), (2 + third, third), (2 + 2 * third, count - 2 - 2 * third), (0, 2))
 
 
 def at_lane(x, lane):
@@ -43,20 +50,26 @@
     return now * r + after(early * r) + before(late * r)
 
 
-def kernel(n, data_hbm, model_hbm, dip_hbm, tents_ref, new_model, new_res,
-           data, model, dip, res, grad, halo, sums_out, sums_in, split, shaped, image,
+def kernel(n, data_hbm, model_hbm, dip_hbm, new_model, new_res,
+           data, model, dip, res, grad, halo, sums_out, sums_in, split, tents, tents_last, shaped, image,
            below, above, above_dip, part, table, part_two, table_two,
            load_sem, edge_send, edge_recv, near_send, near_recv, far_send, far_recv,
            sum_send, sum_recv, one_send, one_recv, two_send, two_recv):
     count, columns, _ = data.shape
+    cuts = pieces(count)
+
+    def slot(i):
+        return (i + 1) % count
+
     width = columns // PARTS
-    groups = n // 8
+    size = min(GROUP, n)
+    groups = n // size
     me = lax.axis_index("il")
-    pos = lax.rem(me, 8)
-    group = lax.div(me, 8)
-    side = lax.div(pos, 4)
-    place = lax.rem(pos, 4)
-    base8 = me - pos
+    pos = lax.rem(me, size)
+    group = lax.div(me, size)
+    side = lax.rem(lax.div(me, 4), 2)
+    place = lax.rem(me, 4)
+    base = me - pos
     base4 = me - place
     toward = 1 - 2 * side
     partner = me + 4 * toward
@@ -83,12 +96,12 @@
         pl.semaphore_signal(barrier, inc=1, device_id={"il": other},
                             device_id_type=pl.DeviceIdType.MESH)
 
-    for o in range(1, 8):
-        greet(base8 + lax.rem(pos + o, 8))
+    for o in range(1, size):
+        greet(base + lax.rem(pos + o, size))
     for o in range(1, groups):
-        greet(lax.rem(me + 8 * o, n))
+        greet(lax.rem(me + size * o, n))
     cross_below = jnp.logical_and(pos == 0, has_below)
-    cross_above = jnp.logical_and(pos == 7, has_above)
+    cross_above = jnp.logical_and(pos == size - 1, has_above)
 
     @pl.when(cross_below)
     def _():
@@ -99,7 +112,7 @@
         greet(me + 1)
 
     crossings = cross_below.astype(jnp.int32) + cross_above.astype(jnp.int32)
-    pl.semaphore_wait(barrier, 7 + groups - 1 + crossings)
+    pl.semaphore_wait(barrier, size - 1 + groups - 1 + crossings)
 
     def up():
         return [remote(model_hbm.at[count - 1], below, edge_send.at[0], edge_recv.at[0], me + 1)]
@@ -119,11 +132,44 @@
         for copy in down():
             copy.start()
 
+    def tent_weights(first, shape):
+        row = lax.broadcasted_iota(jnp.int32, shape, 0)
+        lane = lax.broadcasted_iota(jnp.int32, shape, 1) + first
+        column = (lane // (2 * width)) * width + lane % width
+        weight = jnp.maximum(RAD - jnp.abs(row - column), 0).astype(jnp.float32)
+        return (weight * (1.0 / float(RAD) ** 4)).astype(jnp.bfloat16)
+
+    last_strip = 2 * (columns - width)
+    tents[...] = tent_weights(0, tents.shape)
+    tents_last[...] = tent_weights(last_strip, tents_last.shape)
+    for i in range(count + 1):
+        split[i, pl.ds(last_strip, 2 * width)] = jnp.zeros((2 * width, split.shape[2]), split.dtype)
+
     for load in loads:
         load.wait()
 
     def strip(k):
         return pl.ds(pl.multiple_of(k * width, width), width)
+
+    def rows(h):
+        return pl.ds(*cuts[h])
+
+    def near(k, h):
+        return remote(grad.at[rows(h), strip(k)], halo.at[side, rows(h), strip(k)],
+                      near_send.at[k, h], near_recv.at[k, h], partner)
+
+    def near_arrival(k, h):
+        return remote(grad.at[rows(h), strip(k)], halo.at[1 - side, rows(h), strip(k)],
+                      near_send.at[k, h], near_recv.at[k, h], partner)
+
+    def far(k, h):
+        return remote(halo.at[1 - side, rows(h), strip(k)], halo.at[side, rows(h), strip(k)],
+                      far_send.at[k, h], far_recv.at[k, h], onward)
+
+    def moments(o, k):
+        return remote(sums_out.at[o - 1, :, strip(k)], sums_in.at[o - 1, :, strip(k)],
+                      sum_send.at[o - 1, k], sum_recv.at[o - 1, k],
+                      base4 + lax.rem(place + o, 4))
 
     def own(k, carry):
         xs = strip(k)
@@ -133,9 +179,14 @@
             r = data[i, xs] - model[i, xs] + predict(model[i - 1, xs], weights)
             res[i, xs] = r
             s = spread(r, weights)
-            grad[i - 1, xs] = -s if last is None else last - s
+            grad[slot(i - 1), xs] = -s if last is None else last - s
             last = r
-        grad[count - 1, xs] = last
+        grad[slot(count - 1), xs] = last
+
+        @pl.when(k < EARLY)
+        def _():
+            for h in range(PIECES - 1):
+                near(k, h).start()
         return carry
 
     lax.fori_loop(0, PARTS, own, 0)
@@ -158,33 +209,21 @@
         xs = strip(k)
         r = data[0, xs] - model[0, xs] + predict(below[xs], coefficients(dip[0, xs]))
         res[0, xs] = r
-        grad[0, xs] = grad[0, xs] + r
+        grad[slot(0), xs] = grad[slot(0), xs] + r
 
         @pl.when(has_above)
         def _():
             weights = coefficients(above_dip[xs])
             r = above[0, xs] - above[1, xs] + predict(model[count - 1, xs], weights)
-            grad[count - 1, xs] = grad[count - 1, xs] - spread(r, weights)
-
-        near(k).start()
-        return carry
-
-    def near(k):
-        return remote(grad.at[:, strip(k)], halo.at[side, :, strip(k)],
-                      near_send.at[k], near_recv.at[k], partner)
-
-    def near_arrival(k):
-        return remote(grad.at[:, strip(k)], halo.at[1 - side, :, strip(k)],
-                      near_send.at[k], near_recv.at[k], partner)
-
-    def far(k):
-        return remote(halo.at[1 - side, :, strip(k)], halo.at[side, :, strip(k)],
-                      far_send.at[k], far_recv.at[k], onward)
-
-    def moments(o, k):
-        return remote(sums_out.at[o - 1, :, strip(k)], sums_in.at[o - 1, :, strip(k)],
-                      sum_send.at[o - 1, k], sum_recv.at[o - 1, k],
-                      base4 + lax.rem(place + o, 4))
+            grad[slot(count - 1), xs] = grad[slot(count - 1), xs] - spread(r, weights)
+
+        near(k, PIECES - 1).start()
+
+        @pl.when(k >= EARLY)
+        def _():
+            for h in range(PIECES - 1):
+                near(k, h).start()
+        return carry
 
     lax.fori_loop(0, PARTS, edges, 0)
 
@@ -207,9 +246,9 @@
 
     def send_moments(k):
         xs = strip(k)
-        left0, left1 = totals([halo[0, j, xs] for j in range(count)])
-        own0, own1 = totals([grad[j, xs] for j in range(count)])
-        right0, right1 = totals([halo[1, j, xs] for j in range(count)])
+        left0, left1 = totals([halo[0, slot(j), xs] for j in range(count)])
+        own0, own1 = totals([grad[slot(j), xs] for j in range(count)])
+        right0, right1 = totals([halo[1, slot(j), xs] for j in range(count)])
         for o in range(1, 4):
             wrap = place + o >= 4
             a0 = jnp.where(wrap, left0, own0)
@@ -231,34 +270,37 @@
         for o in range(3):
             value = value + sums_in[o, 0, xs]
             step = step + sums_in[o, 1, xs]
-        low = pl.ds(pl.multiple_of(columns + k * width, width), width)
+        top = pl.ds(pl.multiple_of(2 * k * width, width), width)
+        low = pl.ds(pl.multiple_of((2 * k + 1) * width, width), width)
 
         def put(i, v):
             high = v.astype(jnp.bfloat16)
-            split[i, xs] = high
+            split[i, top] = high
             split[i, low] = (v - high.astype(jnp.float32)).astype(jnp.bfloat16)
 
         put(0, value - step)
         for i in range(count):
             put(i + 1, value)
             if i < count - 1:
-                step = step + ((halo[0, i, xs] + halo[1, i, xs]) - 2.0 * grad[i, xs])
+                step = step + ((halo[0, slot(i), xs] + halo[1, slot(i), xs]) - 2.0 * grad[slot(i), xs])
                 value = value + step
 
     def stage(k, carry):
         @pl.when(k < PARTS)
         def _():
-            near_arrival(k).wait_recv()
-
-            @pl.when(has_onward)
-            def _():
-                far(k).start()
+            for h in range(PIECES):
+                near_arrival(k, h).wait_recv()
+
+                @pl.when(has_onward)
+                def _():
+                    far(k, h).start()
 
         @pl.when(jnp.logical_and(k >= 1, k <= PARTS))
         def _():
             @pl.when(has_origin)
             def _():
-                far(k - 1).wait_recv()
+                for h in range(PIECES):
+                    far(k - 1, h).wait_recv()
             send_moments(k - 1)
 
         @pl.when(k >= 2)
@@ -266,14 +308,23 @@
             smooth(k - 2)
         return carry
 
-    lax.fori_loop(0, PARTS + 2, stage, 0)
+    lax.fori_loop(0, PARTS + 1, stage, 0)
 
     def across(i, carry):
-        out = jnp.dot(tents_ref[...], split[i], preferred_element_type=jnp.float32)
+        shaped[i] = jnp.dot(tents[...], split[i], preferred_element_type=jnp.float32)
+        return carry
+
+    lax.fori_loop(0, count + 1, across, 0, unroll=True)
+    smooth(PARTS - 1)
+
+    def across_last(i, carry):
+        more = jnp.dot(tents_last[...], split[i, pl.ds(last_strip, 2 * width)],
+                       preferred_element_type=jnp.float32)
+        out = shaped[i] + more
         shaped[i] = jnp.where(jnp.logical_or(i > 0, has_below), out, 0.0)
         return carry
 
-    lax.fori_loop(0, count + 1, across, 0)
+    lax.fori_loop(0, count + 1, across_last, 0, unroll=True)
 
     def fold(x):
         return jnp.sum(x.reshape(x.shape[0] // 8, 8, x.shape[1]), 0)
@@ -286,7 +337,7 @@
             now = shaped[i + 1, xs]
             im = now - predict(last, coefficients(dip[i, xs]))
             image[i, xs] = im
-            along = along + fold(grad[i, xs] * now)
+            along = along + fold(grad[slot(i), xs] * now)
             energy = energy + fold(im * im)
             length = length + fold(now * now)
             last = now
@@ -305,26 +356,26 @@
 
     def one(o):
         return remote(part, table.at[pos], one_send.at[o - 1], one_recv.at[o - 1],
-                      base8 + lax.rem(pos + o, 8))
+                      base + lax.rem(pos + o, size))
 
     def one_arrival(o):
-        return remote(part, table.at[lax.rem(pos + 8 - o, 8)], one_send.at[o - 1],
-                      one_recv.at[o - 1], base8 + lax.rem(pos + o, 8))
+        return remote(part, table.at[lax.rem(pos + size - o, size)], one_send.at[o - 1],
+                      one_recv.at[o - 1], base + lax.rem(pos + o, size))
 
     def two(o):
         return remote(part_two, table_two.at[group], two_send.at[o - 1], two_recv.at[o - 1],
-                      lax.rem(me + 8 * o, n))
+                      lax.rem(me + size * o, n))
 
     def two_arrival(o):
         return remote(part_two, table_two.at[lax.rem(group + groups - o, groups)],
-                      two_send.at[o - 1], two_recv.at[o - 1], lax.rem(me + 8 * o, n))
-
-    for o in range(1, 8):
+                      two_send.at[o - 1], two_recv.at[o - 1], lax.rem(me + size * o, n))
+
+    for o in range(1, size):
         one(o).start()
-    for o in range(1, 8):
+    for o in range(1, size):
         one_arrival(o).wait_recv()
     tile = table[0]
-    for o in range(1, 8):
+    for o in range(1, size):
         tile = tile + table[o]
     part_two[...] = tile
     table_two[group] = tile
@@ -356,17 +407,19 @@
             copy.wait_send()
 
     def finish(k, carry):
-        near(k).wait_send()
+        for h in range(PIECES):
+            near(k, h).wait_send()
 
         @pl.when(has_onward)
         def _():
-            far(k).wait_send()
+            for h in range(PIECES):
+                far(k, h).wait_send()
         for o in range(1, 4):
             moments(o, k).wait_send()
         return carry
 
     lax.fori_loop(0, PARTS, finish, 0)
-    for o in range(1, 8):
+    for o in range(1, size):
         one(o).wait_send()
     for o in range(1, groups):
         two(o).wait_send()
@@ -375,18 +428,16 @@
 def local(n, data, model, dip):
     count, columns, times = data.shape
     assert count * 4 == RAD and n % 8 == 0
-    groups = n // 8
-    gap = np.abs(np.arange(columns)[:, None] - np.arange(columns)[None, :])
-    tent = np.maximum(RAD - gap, 0) / float(RAD) ** 4
-    tents = jnp.asarray(np.concatenate([tent, tent], 1), jnp.bfloat16)
+    size = min(GROUP, n)
+    groups = n // size
+    width = columns // PARTS
     block = (count, columns, times)
     f32 = jnp.float32
     dma = pltpu.SemaphoreType.DMA
     return pl.pallas_call(
         functools.partial(kernel, n),
         out_shape=[jax.ShapeDtypeStruct(block, f32)] * 2,
-        in_specs=[pl.BlockSpec(memory_space=pl.ANY)] * 3
-        + [pl.BlockSpec(memory_space=pltpu.VMEM)],
+        in_specs=[pl.BlockSpec(memory_space=pl.ANY)] * 3,
         out_specs=[pl.BlockSpec(memory_space=pltpu.VMEM)] * 2,
         scratch_shapes=[
             pltpu.VMEM(block, f32),
@@ -398,26 +449,28 @@
             pltpu.VMEM((4, 2, columns, times), f32),
             pltpu.VMEM((3, 2, columns, times), f32),
             pltpu.VMEM((count + 1, 2 * columns, times), jnp.bfloat16),
+            pltpu.VMEM((columns, 2 * columns), jnp.bfloat16),
+            pltpu.VMEM((columns, 2 * width), jnp.bfloat16),
             pltpu.VMEM((count + 1, columns, times), f32),
             pltpu.VMEM(block, f32),
             pltpu.VMEM((columns, times), f32),
             pltpu.VMEM((2, columns, times), f32),
             pltpu.VMEM((columns, times), jnp.int32),
             pltpu.VMEM((8, 128), f32),
-            pltpu.VMEM((8, 8, 128), f32),
+            pltpu.VMEM((size, 8, 128), f32),
             pltpu.VMEM((8, 128), f32),
             pltpu.VMEM((groups, 8, 128), f32),
             dma((3,)),
             dma((4,)), dma((4,)),
-            dma((PARTS,)), dma((PARTS,)),
-            dma((PARTS,)), dma((PARTS,)),
+            dma((PARTS, PIECES)), dma((PARTS, PIECES)),
+            dma((PARTS, PIECES)), dma((PARTS, PIECES)),
             dma((3, PARTS)), dma((3, PARTS)),
-            dma((7,)), dma((7,)),
+            dma((size - 1,)), dma((size - 1,)),
             dma((max(groups - 1, 1),)), dma((max(groups - 1, 1),)),
         ],
         compiler_params=pltpu.CompilerParams(
             collective_id=0, has_side_effects=True, vmem_limit_bytes=48 * 2**20),
-    )(data, model, dip, tents)
+    )(data, model, dip)
 
 
 def solution(mesh):

time: 88.2 us -> 80 us (0.907)
  Pallas kernels: 83.9 us -> 76.6 us
    pallas_call x1, Pallas kernels: 83.9 us -> 76.6 us  [local(): pl.pallas_call(functools.partial(kernel, n), out_shape=[jax.ShapeDtypeStr...]
    unnamed x4 -> x2, local copies, waits for them, and re-layouts: 3.48 us -> 2.64 us
where the time goes in v2:
time: 80 us; the launch traced here: 79.9 us
  Pallas kernels  76.6 us (96%)
  local copies, waits for them, and re-layouts  2.64 us (3%)
    pallas_call x1, Pallas kernels, local(): pl.pallas_call(functools.partial(kernel, n), out_shape=[jax.ShapeDtypeStr...  76.6 us
    unnamed x2, local copies, waits for them, and re-layouts  2.64 us

profile of v2, /device:TPU:0, one launch (start us, length us, event | category | flops | bytes accessed | tf_op | source)
XLA Modules:
  0.0 79.9 jit_solution(16226366354466906909)
XLA Ops:
  0.6 76.6 %shard_map.50 = (f32[16,128,256]{2,1,0:T(8,128)S(1)}, f32[16,128,256]{2,1,0:T(8,128)S(1)}) custom-call(f32[16,128,256]{2,1,0:T(8,128)} %data_hbm.1, f32[16,128,256]{2,1,0:T(8,128)} %model_hbm.1, s32[16,128,256]{2,1,0:T(8,128)} %dip_hbm.1), custom_call_target="tpu_custom_call" | custom-call | tf_op jit(solution)/shard_map/pallas_call | solution.py:437
  77.2 1.3 %copy.7 = f32[16,128,256]{2,1,0:T(8,128)} copy(f32[16,128,256]{2,1,0:T(8,128)S(1)} %get-tuple-element.4) | data formatting | bytes 4194304
  78.6 1.3 %copy.8 = f32[16,128,256]{2,1,0:T(8,128)} copy(f32[16,128,256]{2,1,0:T(8,128)S(1)} %get-tuple-element.5) | data formatting | bytes 4194304

commit v3 on v2

--- a/solution.py
+++ b/solution.py
@@ -12,12 +12,12 @@
 PARTS = 8
 GROUP = 8
 EARLY = 1
-PIECES = 4
+PIECES = 3
 
 
 def pieces(count):
-    third = (count - 2 + 2) // 3
-    return ((2, third), (2 + third, third), (2 + 2 * third, count - 2 - 2 * third), (0, 2))
+    half = (count - 2) // 2
+    return ((2, half), (2 + half, count - 2 - half), (0, 2))
 
 
 def at_lane(x, lane):
@@ -85,9 +85,11 @@
             src_ref=src, dst_ref=dst, send_sem=send, recv_sem=recv,
             device_id={"il": to}, device_id_type=pl.DeviceIdType.MESH)
 
-    loads = [pltpu.make_async_copy(src, dst, load_sem.at[i]) for i, (src, dst) in enumerate(
-        ((data_hbm, data), (model_hbm, model), (dip_hbm, dip)))]
-    for load in loads:
+    loads = [[pltpu.make_async_copy(src.at[:, cut], dst.at[:, cut], load_sem.at[i, j])
+              for i, (src, dst) in enumerate(
+                  ((data_hbm, data), (model_hbm, model), (dip_hbm, dip)))]
+             for j, cut in enumerate((pl.ds(0, width), pl.ds(width, columns - width)))]
+    for load in loads[0] + loads[1]:
         load.start()
 
     barrier = pltpu.get_barrier_semaphore()
@@ -145,7 +147,7 @@
     for i in range(count + 1):
         split[i, pl.ds(last_strip, 2 * width)] = jnp.zeros((2 * width, split.shape[2]), split.dtype)
 
-    for load in loads:
+    for load in loads[0]:
         load.wait()
 
     def strip(k):
@@ -183,13 +185,16 @@
             last = r
         grad[slot(count - 1), xs] = last
 
-        @pl.when(k < EARLY)
+        @pl.when(jnp.int32(k) < EARLY)
         def _():
             for h in range(PIECES - 1):
                 near(k, h).start()
         return carry
 
-    lax.fori_loop(0, PARTS, own, 0)
+    own(0, 0)
+    for load in loads[1]:
+        load.wait()
+    lax.fori_loop(1, PARTS, own, 0)
 
     @pl.when(has_below)
     def _():
@@ -344,7 +349,7 @@
         return along, energy, length
 
     none = jnp.zeros((8, data.shape[2]), jnp.float32)
-    sums = lax.fori_loop(0, PARTS, images, (none, none, none))
+    sums = lax.fori_loop(0, PARTS, images, (none, none, none), unroll=2)
     row = lax.broadcasted_iota(jnp.int32, (8, 128), 0)
     tile = jnp.zeros((8, 128), jnp.float32)
     for q, total in enumerate(sums):
@@ -372,6 +377,29 @@
 
     for o in range(1, size):
         one(o).start()
+    @pl.when(has_above)
+    def _():
+        for copy in up():
+            copy.wait_send()
+
+    @pl.when(has_below)
+    def _():
+        for copy in down():
+            copy.wait_send()
+
+    def finish(k, carry):
+        for h in range(PIECES):
+            near(k, h).wait_send()
+
+        @pl.when(has_onward)
+        def _():
+            for h in range(PIECES):
+                far(k, h).wait_send()
+        for o in range(1, 4):
+            moments(o, k).wait_send()
+        return carry
+
+    lax.fori_loop(0, PARTS, finish, 0)
     for o in range(1, size):
         one_arrival(o).wait_recv()
     tile = table[0]
@@ -394,31 +422,8 @@
         new_res[i] = res[i] - alpha * image[i]
         return carry
 
-    lax.fori_loop(0, count, update, 0)
-
-    @pl.when(has_above)
-    def _():
-        for copy in up():
-            copy.wait_send()
-
-    @pl.when(has_below)
-    def _():
-        for copy in down():
-            copy.wait_send()
-
-    def finish(k, carry):
-        for h in range(PIECES):
-            near(k, h).wait_send()
-
-        @pl.when(has_onward)
-        def _():
-            for h in range(PIECES):
-                far(k, h).wait_send()
-        for o in range(1, 4):
-            moments(o, k).wait_send()
-        return carry
-
-    lax.fori_loop(0, PARTS, finish, 0)
+    lax.fori_loop(0, count, update, 0, unroll=4)
+
     for o in range(1, size):
         one(o).wait_send()
     for o in range(1, groups):
@@ -460,7 +465,7 @@
             pltpu.VMEM((size, 8, 128), f32),
             pltpu.VMEM((8, 128), f32),
             pltpu.VMEM((groups, 8, 128), f32),
-            dma((3,)),
+            dma((3, 2)),
             dma((4,)), dma((4,)),
             dma((PARTS, PIECES)), dma((PARTS, PIECES)),
             dma((PARTS, PIECES)), dma((PARTS, PIECES)),

time: 80 us -> 78.5 us (0.981)
  Pallas kernels: 76.6 us -> 75.1 us
    pallas_call x1, Pallas kernels: 76.6 us -> 75.1 us  [local(): pl.pallas_call(functools.partial(kernel, n), out_shape=[jax.ShapeDtypeStr...]
where the time goes in v3:
time: 78.5 us; the launch traced here: 78.4 us
  Pallas kernels  75.1 us (96%)
  local copies, waits for them, and re-layouts  2.64 us (3%)
    pallas_call x1, Pallas kernels, local(): pl.pallas_call(functools.partial(kernel, n), out_shape=[jax.ShapeDtypeStr...  75.1 us
    unnamed x2, local copies, waits for them, and re-layouts  2.64 us

profile of v3, /device:TPU:0, one launch (start us, length us, event | category | flops | bytes accessed | tf_op | source)
XLA Modules:
  0.0 78.4 jit_solution(8547192898151793743)
XLA Ops:
  0.6 75.1 %shard_map.50 = (f32[16,128,256]{2,1,0:T(8,128)S(1)}, f32[16,128,256]{2,1,0:T(8,128)S(1)}) custom-call(f32[16,128,256]{2,1,0:T(8,128)} %data_hbm.1, f32[16,128,256]{2,1,0:T(8,128)} %model_hbm.1, s32[16,128,256]{2,1,0:T(8,128)} %dip_hbm.1), custom_call_target="tpu_custom_call" | custom-call | tf_op jit(solution)/shard_map/pallas_call | solution.py:442
  75.7 1.3 %copy.7 = f32[16,128,256]{2,1,0:T(8,128)} copy(f32[16,128,256]{2,1,0:T(8,128)S(1)} %get-tuple-element.4) | data formatting | bytes 4194304
  77.0 1.3 %copy.8 = f32[16,128,256]{2,1,0:T(8,128)} copy(f32[16,128,256]{2,1,0:T(8,128)S(1)} %get-tuple-element.5) | data formatting | bytes 4194304

commit v4 on v3

--- a/solution.py
+++ b/solution.py
@@ -12,12 +12,12 @@
 PARTS = 8
 GROUP = 8
 EARLY = 1
-PIECES = 3
+PIECES = 4
 
 
 def pieces(count):
-    half = (count - 2) // 2
-    return ((2, half), (2 + half, count - 2 - half), (0, 2))
+    third = count // 3
+    return ((2, third), (2 + third, third), (2 + 2 * third, count - 2 - 2 * third), (0, 2))
 
 
 def at_lane(x, lane):
@@ -222,12 +222,12 @@
             r = above[0, xs] - above[1, xs] + predict(model[count - 1, xs], weights)
             grad[slot(count - 1), xs] = grad[slot(count - 1), xs] - spread(r, weights)
 
-        near(k, PIECES - 1).start()
-
         @pl.when(k >= EARLY)
         def _():
             for h in range(PIECES - 1):
                 near(k, h).start()
+
+        near(k, PIECES - 1).start()
         return carry
 
     lax.fori_loop(0, PARTS, edges, 0)

time: 78.5 us -> 79 us (level)
  no operation moved by 1% of the time
where the time goes in v4:
time: 79 us; the launch traced here: 78.8 us
  Pallas kernels  75.5 us (96%)
  local copies, waits for them, and re-layouts  2.64 us (3%)
    pallas_call x1, Pallas kernels, local(): pl.pallas_call(functools.partial(kernel, n), out_shape=[jax.ShapeDtypeStr...  75.5 us
    unnamed x2, local copies, waits for them, and re-layouts  2.64 us

profile of v4, /device:TPU:0, one launch (start us, length us, event | category | flops | bytes accessed | tf_op | source)
XLA Modules:
  0.0 78.8 jit_solution(7070969463454561051)
XLA Ops:
  0.6 75.5 %shard_map.50 = (f32[16,128,256]{2,1,0:T(8,128)S(1)}, f32[16,128,256]{2,1,0:T(8,128)S(1)}) custom-call(f32[16,128,256]{2,1,0:T(8,128)} %data_hbm.1, f32[16,128,256]{2,1,0:T(8,128)} %model_hbm.1, s32[16,128,256]{2,1,0:T(8,128)} %dip_hbm.1), custom_call_target="tpu_custom_call" | custom-call | tf_op jit(solution)/shard_map/pallas_call | solution.py:442
  76.2 1.3 %copy.7 = f32[16,128,256]{2,1,0:T(8,128)} copy(f32[16,128,256]{2,1,0:T(8,128)S(1)} %get-tuple-element.4) | data formatting | bytes 4194304
  77.5 1.3 %copy.8 = f32[16,128,256]{2,1,0:T(8,128)} copy(f32[16,128,256]{2,1,0:T(8,128)S(1)} %get-tuple-element.5) | data formatting | bytes 4194304
